TPU v7x, 32 devices: a whole 2x2x4 slice. The times are simulated.
32 devices in a mesh: groups: 1, expert: 8 (over z, y), head: 2 (over x), pair: 2 (over core).
Axes of the slice: x: 2, y: 2, z: 4, core: 2. Of those that a mesh axis runs over, the one named last changes fastest.
Arguments:
- hidden: bfloat16 [512, 4096], P(('groups', 'expert', 'pair'), 'head'), may hold values from -6 to 6
- expert_ids: int32 [512, 8], P(('groups', 'expert', 'pair')), may hold values from 0 to 15, all different within a row; in each aligned block of 32 rows (0 to 31, 32 to 63, ...) at most 32 rows name the same one
- route_weights: float32 [512, 8], P(('groups', 'expert', 'pair')), may hold values from 0.05 to 1
- w_gate: bfloat16 [16, 4096, 1024], P(('expert', 'pair'), None, 'head'), may hold values from -0.09375 to 0.09375
- w_up: bfloat16 [16, 4096, 1024], P(('expert', 'pair'), None, 'head'), may hold values from -0.09375 to 0.09375
- w_down: bfloat16 [16, 1024, 4096], P(('expert', 'pair'), 'head'), may hold values from -0.1875 to 0.1875
Outputs:
- moe_out: bfloat16 [512, 4096], P(('groups', 'expert', 'pair'), 'head')
Inputs may be any that keep to these rules, and one draw needn't show every extreme that they name: `expert_ids`: in each aligned block of 32 rows (the rows of one device) no expert is named by more than 32 rows, a bound that some block reaches. A row names 8 different experts.
All inputs are finite; a program needn't handle non-finite values.
Results may differ from a plain program's by a relative error of at most 0.0085.
Values may be sent and summed in bfloat16 or wider, within the bound.
A program may use at most 64 MiB of HBM per device.

v0:
```python
import jax
import jax.numpy as jnp
from jax import lax
from jax.sharding import PartitionSpec as P


def route_tables(expert_ids, experts, capacity):
    row_count, top_count = expert_ids.shape
    flat_ids = expert_ids.reshape(row_count * top_count)
    one_hot = (flat_ids[:, None] == jnp.arange(experts, dtype=jnp.int32)[None, :]).astype(jnp.int32)
    earlier = jnp.cumsum(one_hot, axis=0) - one_hot
    slot_index = jnp.sum(earlier * one_hot, axis=1)
    position = flat_ids * capacity + slot_index
    placed = (position[:, None] == jnp.arange(experts * capacity, dtype=jnp.int32)[None, :]).astype(
        jnp.float32
    )
    owners = jnp.arange(row_count * top_count, dtype=jnp.int32) // top_count
    picker = (owners[:, None] == jnp.arange(row_count, dtype=jnp.int32)[None, :]).astype(
        jnp.float32
    )
    chooser = jnp.dot(placed.T, picker, precision=lax.Precision.HIGHEST)
    return (chooser.astype(jnp.bfloat16), position)


def weigh_routes(returned, position, route_weights):
    row_count, top_count = route_weights.shape
    slots = returned.reshape(position.shape[0] * 0 + returned.shape[0] * returned.shape[1], -1)
    picked = slots[position]
    picked = picked.reshape(row_count, top_count, -1) * route_weights[:, :, None]
    return jnp.sum(picked, axis=1)


def body(hidden, expert_ids, route_weights, w_gate, w_up, w_down):
    row_count, local_width = hidden.shape
    top_count = expert_ids.shape[1]
    experts = lax.axis_size(("expert", "pair"))
    capacity = min(row_count, 2 * row_count * top_count // experts)
    chooser, position = route_tables(expert_ids, experts, capacity)
    gate_weight = w_gate[0]
    up_weight = w_up[0]
    down_weight = w_down[0]
    outgoing = jnp.dot(chooser, hidden, preferred_element_type=jnp.float32).astype(jnp.bfloat16)
    outgoing = outgoing.reshape(experts, capacity, local_width)
    incoming = lax.all_to_all(outgoing, ("expert", "pair"), split_axis=0, concat_axis=0, tiled=True)
    segment = lax.all_gather(incoming, "head", axis=2, tiled=True)
    gate_next = jnp.einsum("scd,df->scf", segment, gate_weight, preferred_element_type=jnp.float32)
    up_next = jnp.einsum("scd,df->scf", segment, up_weight, preferred_element_type=jnp.float32)
    activated = (jax.nn.silu(gate_next) * up_next).astype(jnp.bfloat16)
    partials = jnp.einsum(
        "scf,fd->scd", activated, down_weight, preferred_element_type=jnp.float32
    ).astype(jnp.bfloat16)
    summed = lax.psum_scatter(partials, "head", scatter_dimension=2, tiled=True).astype(jnp.float32)
    returned = lax.all_to_all(
        summed.astype(jnp.bfloat16), ("expert", "pair"), split_axis=0, concat_axis=0, tiled=True
    ).astype(summed.dtype)
    combined = weigh_routes(returned, position, route_weights)
    return combined.astype(jnp.bfloat16)


def solution(mesh):
    return jax.shard_map(
        body,
        mesh=mesh,
        in_specs=(
            P(("groups", "expert", "pair"), "head"),
            P(("groups", "expert", "pair"), None),
            P(("groups", "expert", "pair"), None),
            P(("expert", "pair"), None, "head"),
            P(("expert", "pair"), None, "head"),
            P(("expert", "pair"), "head", None),
        ),
        out_specs=P(("groups", "expert", "pair"), "head"),
        check_vma=False,
    )
```

profile of v0, /device:TPU:13, one launch (start us, length us, event | category | flops | bytes accessed | tf_op | source)
XLA Modules:
  0.0 260.7 jit_solution(1092501685645694745)
XLA Ops:
  6.5 0.0 copy-start
  6.5 0.0 all-gather.2.cloned.1.call-start
  6.5 0.8 copy.8
  7.3 0.1 eq.52
  7.4 0.1 reshape.79
  7.5 0.6 reduce-window.6
  8.1 0.2 slice_reduce_fusion
  8.3 0.1 fusion.19
  8.4 0.4 convolution_convert_fusion.2
  8.9 0.0 copy-done
  8.9 0.7 convolution_convert_fusion.1
  9.6 53.8 %all_to_all.10 = bf16[16,32,2048]{2,1,0:T(8,128)(2,1)} all-to-all(bf16[16,32,2048]{2,1,0:T(8,128)(2,1)S(1)} %bitcast.51), channel_id=1, replica_groups=mesh['groups'=1,'expert'=8,'head'=2,'pair'=2] {'expert','pair'}, dimensions={0} | all-to-all | bytes 4194304 | tf_op jit(solution)/shard_map/all_to_all | solution.py:44
  63.4 0.0 all-gather.2.cloned.1.call-update
  63.4 0.0 reduce-scatter.2.cloned.1.call-start
  63.4 56.5 %all-gather.2.cloned.1.call-done = bf16[16,32,4096]{2,1,0:T(8,128)(2,1)} async-done(((bf16[16,32,2048]{2,1,0:T(8,128)(2,1)}), bf16[16,32,4096]{2,1,0:T(8,128)(2,1)}) %all-gather.2.cloned.1.call-update) | async-done | bytes 4194320 | tf_op jit(solution)/shard_map/all_gather | solution.py:45
  120.0 5.8 %fusion.3 = f32[16,32,512]{2,1,0:T(8,128)S(1)} fusion(bf16[16,32,4096]{2,1,0:T(8,128)(2,1)} %all-gather.2.cloned.1.call-done, bf16[1,4096,512]{2,1,0:T(8,128)(2,1)} %param.9), kind=kOutput, calls=%fused_computation.5 | convolution fusion | flops 2147483648 | bytes 9437184 | tf_op jit(solution)/shard_map/scd,df->scf/dot_general | solution.py:46
  125.8 11.3 %convolution_convert_fusion = bf16[16,32,4096]{2,1,0:T(8,128)(2,1)} fusion(bf16[1,512,4096]{2,1,0:T(8,128)(2,1)} %param.11, bf16[16,32,4096]{2,1,0:T(8,128)(2,1)} %all-gather.2.cloned.1.call-done, bf16[1,4096,512]{2,1,0:T(8,128)(2,1)} %param.10, f32[16,32,512]{2,1,0:T(8,128)S(1)} %fusion.3), kind=kOutput, calls=%fused_computation.1 | convolution fusion | flops 4298637312 | bytes 17825792 | tf_op jit(solution)/shard_map/scf,fd->scd/dot_general | solution.py:49
  137.0 0.0 copy-start.1
  137.0 0.0 copy-start.2
  137.0 0.0 reduce-scatter.2.cloned.1.call-update
  137.1 54.5 %reduce-scatter.2.cloned.1.call-done = bf16[16,32,2048]{2,1,0:T(8,128)(2,1)} async-done(((bf16[16,32,4096]{2,1,0:T(8,128)(2,1)}), bf16[16,32,2048]{2,1,0:T(8,128)(2,1)}) %reduce-scatter.2.cloned.1.call-update) | async-done | bytes 2097168 | tf_op jit(solution)/shard_map/reduce_scatter | solution.py:52
  191.5 6.3 %all-to-all-start.1 = ((bf16[16,32,2048]{2,1,0:T(8,128)(2,1)}), bf16[16,32,2048]{2,1,0:T(8,128)(2,1)S(1)}, u32[]{:S(2)}, u32[]{:S(2)}) async-start(bf16[16,32,2048]{2,1,0:T(8,128)(2,1)} %reduce-scatter.2.cloned.1.call-done), calls=%async_computation.2 | async-start | bytes 4194304 | tf_op jit(solution)/shard_map/all_to_all | solution.py:53
  197.9 0.0 copy-done.1
  197.9 0.1 copy.11
  198.0 0.1 mul.48
  198.1 0.0 copy-done.2
  198.1 0.1 copy.12
  198.2 47.1 %all-to-all-done.1 = bf16[16,32,2048]{2,1,0:T(8,128)(2,1)S(1)} async-done(((bf16[16,32,2048]{2,1,0:T(8,128)(2,1)}), bf16[16,32,2048]{2,1,0:T(8,128)(2,1)S(1)}, u32[]{:S(2)}, u32[]{:S(2)}) %all-to-all-start.1) | async-done | bytes 2097184 | tf_op jit(solution)/shard_map/all_to_all | solution.py:53
  245.3 2.6 bitcast_convert_fusion
  247.9 4.6 %gather_fusion = f32[256,2048]{1,0:T(8,128)S(1)} fusion(f32[512,2048]{1,0:T(8,128)} %bitcast_convert_fusion, s32[1024]{0:T(1024)S(1)} %pad_clamp_fusion), kind=kCustom, calls=%fused_computation | custom fusion | bytes 4195328 | tf_op jit(solution)/shard_map/gather | solution.py:28
  252.5 1.4 fusion.5
  (7 shorter events, 0.1 us)
Async XLA Ops:
  6.5 2.4 copy-start
  6.5 113.4 %all-gather.2.cloned.1.call-start = ((), (), s32[]{:S(2)}) async-start(), calls=%async_computation.3 | async-start | bytes 6291456 | tf_op jit(solution)/shard_map/all_gather | solution.py:45
  63.4 128.2 %reduce-scatter.2.cloned.1.call-start = ((), (), s32[]{:S(2)}) async-start(), calls=%async_computation.4 | async-start | bytes 6291456 | tf_op jit(solution)/shard_map/reduce_scatter | solution.py:52
  137.0 60.9 %copy-start.1 = (s32[32,8]{0,1:T(8,128)S(1)}, s32[32,8]{0,1:T(8,128)}, u32[]{:S(2)}) copy-start(s32[32,8]{0,1:T(8,128)} %param.7) | copy-start | bytes 3076
  137.0 61.0 %copy-start.2 = (f32[32,8]{0,1:T(8,128)S(1)}, f32[32,8]{0,1:T(8,128)}, u32[]{:S(2)}) copy-start(f32[32,8]{0,1:T(8,128)} %param.8) | copy-start | bytes 3076
  191.5 53.8 %all-to-all-start.1 = ((bf16[16,32,2048]{2,1,0:T(8,128)(2,1)}), bf16[16,32,2048]{2,1,0:T(8,128)(2,1)S(1)}, u32[]{:S(2)}, u32[]{:S(2)}) async-start(bf16[16,32,2048]{2,1,0:T(8,128)(2,1)} %reduce-scatter.2.cloned.1.call-done), calls=%async_computation.2 | async-start | bytes 4194304 | tf_op jit(solution)/shard_map/all_to_all | solution.py:53
Sparse Core Ops, SparseCore 0:
  63.5 56.4 all-gather.1
  137.2 54.3 reduce-scatter.1
where the time goes:
time: 261 us
  waiting for transfers between devices  158 us (61%)
  blocking collectives  53.8 us (21%)
  matrix products  18.2 us (7%)
  between operations  13.5 us (5%)
  starting transfers between devices  6.39 us (2%)
  local copies, waits for them, and re-layouts  5.99 us (2%)
  other arithmetic  4.69 us (2%)
    all_gather x1, waiting for transfers between devices, body(): segment = lax.all_gather(incoming, 'head', axis=2, tiled=True)  56.5 us
    reduce_scatter x1, waiting for transfers between devices, body(): lax.psum_scatter(partials, 'head', scatter_dimension=2, tiled=True)  54.5 us
    all_to_all x1, blocking collectives, body(): lax.all_to_all(outgoing, ('expert', 'pair'), split_axis=0, concat_axis=0,...  53.8 us
    all_to_all x1, waiting for transfers between devices, body(): lax.all_to_all(summed.astype(jnp.bfloat16), ('expert', 'pair'), split_axi...  47.1 us
    dot_general x1, matrix products, body(): jnp.einsum('scf,fd->scd', activated, down_weight, preferred_element_type=...  11.3 us
    all_to_all x1, starting transfers between devices, body(): lax.all_to_all(summed.astype(jnp.bfloat16), ('expert', 'pair'), split_axi...  6.35 us
    dot_general x1, matrix products, body(): jnp.einsum('scd,df->scf', segment, gate_weight, preferred_element_type=jn...  5.79 us
  transfers between devices with their start and end apart: 3, of which 3 were waited for; matrix products, arithmetic and copies ran while one was open for 0% of the time, Pallas kernels for 0%

commit v1 on v0

v1 whole, which is shorter than its diff:
```python
import functools

import jax
import jax.numpy as jnp
from jax import lax
from jax.experimental import pallas as pl
from jax.experimental.pallas import tpu as pltpu
from jax.sharding import PartitionSpec as P

MESH = pl.DeviceIdType.MESH
LANES = 128


def flip(value, bits):
    result = value
    bit = 1
    while bit <= bits:
        if bits & bit:
            result = result + bit * (1 - 2 * ((value // bit) % 2))
        bit *= 2
    return result


def kernel(
    dims, hidden, ids, weights, gate_hbm, up_hbm, down_hbm, out,
    rows_all, table, w_gate, w_up, w_down, part, act, d2d_in, y_in, x_in, x_in2, y_in2, z_out, z_in,
    w_sem, send_sem, recv_sem,
):
    Z, H, RB = dims
    RC = 4 * RB
    WD = rows_all.shape[3]
    expert = lax.axis_index("expert")
    x = lax.axis_index("head")
    c = lax.axis_index("pair")
    z, y = expert // 2, expert % 2
    other = 1 - c
    me = expert * 2 + c

    to_y = {"expert": z * 2 + 1 - y}
    to_c = {"pair": other}

    def to_z(j):
        return {"expert": flip(z, j) * 2 + y}

    def to_x(dx):
        return {"head": (x + dx) % H}

    def from_x(dx):
        return (x + H - dx) % H

    fetches = [
        pltpu.make_async_copy(gate_hbm.at[0], w_gate, w_sem.at[0]),
        pltpu.make_async_copy(up_hbm.at[0], w_up, w_sem.at[1]),
    ]
    for s in range(2 * H):
        fetches.append(
            pltpu.make_async_copy(
                down_hbm.at[0, :, pl.ds(s * WD, WD)], w_down.at[s // 2, s % 2], w_sem.at[2 + s]
            )
        )
    for f in fetches:
        f.start()

    def block(zc, pair, yy):
        return pl.multiple_of(((zc * 2 + pair) * 2 + yy) * RB, RB)

    own = block(z, c, y)
    for p in range(2):
        rows_all[x, p, pl.ds(own, RB), :] = hidden[:, p * WD:(p + 1) * WD]
    lane = lax.broadcasted_iota(jnp.int32, (RB, LANES), 1)
    total = jnp.zeros((RB, LANES), jnp.float32)
    for k in range(ids.shape[1]):
        total = total + jnp.where(lane == ids[:, k:k + 1], weights[:, k:k + 1], 0.0)
    table[pl.ds(own, RB), :] = total

    barrier = pltpu.get_barrier_semaphore()
    peers = [to_c, to_y] + [to_z(j) for j in range(1, Z)] + [to_x(d) for d in range(1, H)]
    for peer in peers:
        pl.semaphore_signal(barrier, inc=1, device_id=peer, device_id_type=MESH)
    pl.semaphore_wait(barrier, len(peers))

    sent = []

    def send(src, dst, peer):
        i = len(sent)
        copy = pltpu.make_async_remote_copy(
            src_ref=src, dst_ref=dst, send_sem=send_sem.at[i], recv_sem=recv_sem.at[i],
            device_id=peer, device_id_type=MESH,
        )
        copy.start()
        sent.append(copy)
        return copy

    def same(ref, peer):
        return send(ref, ref, peer)

    got = {}

    for j in range(1, Z):
        got["z", j] = same(rows_all.at[x, :, pl.ds(own, RB), :], to_z(j))
        got["zw", j] = same(table.at[pl.ds(own, RB), :], to_z(j))

    def g_start(j):
        zc = flip(z, j)
        mine = block(zc, c, y)
        if j:
            got["z", j].wait_recv()
        for d in range(1, H):
            got["x", j, d] = same(rows_all.at[x, :, pl.ds(mine, RB), :], to_x(d))
        got["y", j] = same(rows_all.at[x, :, pl.ds(mine, RB), :], to_y)
        if j:
            got["zw", j].wait_recv()
        got["yw", j] = same(table.at[pl.ds(mine, RB), :], to_y)

    def g_forward(j):
        zc = flip(z, j)
        mine, theirs = block(zc, c, y), block(zc, c, 1 - y)
        for d in range(1, H):
            got["x", j, d].wait_recv()
            got["xy", j, d] = same(rows_all.at[from_x(d), 0, pl.ds(mine, RB), :], to_y)
        got["y", j].wait_recv()
        for d in range(1, H):
            got["yx", j, d] = same(rows_all.at[x, 1, pl.ds(theirs, RB), :], to_x(d))

    def g_pair(j):
        zc = flip(z, j)
        half = block(zc, c, 0)
        for d in range(1, H):
            got["xy", j, d].wait_recv()
            got["yx", j, d].wait_recv()
        got["yw", j].wait_recv()
        got["c", j] = same(rows_all.at[:, :, pl.ds(half, 2 * RB), :], to_c)
        got["cw", j] = same(table.at[pl.ds(half, 2 * RB), :], to_c)

    def compute(j):
        zc = flip(z, j)
        start = block(zc, 0, 0)
        got["c", j].wait_recv()
        got["cw", j].wait_recv()
        if j == 0:
            fetches[0].wait()
            fetches[1].wait()
        gate = jnp.zeros((RC, w_gate.shape[1]), jnp.float32)
        up = gate
        for s in range(2 * H):
            a = rows_all[s // 2, s % 2, pl.ds(start, RC), :]
            gate = gate + jnp.dot(a, w_gate[s * WD:(s + 1) * WD, :], preferred_element_type=jnp.float32)
            up = up + jnp.dot(a, w_up[s * WD:(s + 1) * WD, :], preferred_element_type=jnp.float32)
        act[...] = (gate / (1.0 + jnp.exp(-gate)) * up).astype(jnp.bfloat16)
        if j == 0:
            for f in fetches[2:]:
                f.wait()
        lanes = lax.broadcasted_iota(jnp.int32, (RC, LANES), 1)
        scale = jnp.sum(jnp.where(lanes == me, table[pl.ds(start, RC), :], 0.0), axis=1, keepdims=True)
        for s in range(2 * H):
            o = jnp.dot(act[...], w_down[s // 2, s % 2], preferred_element_type=jnp.float32)
            part[j, s // 2, s % 2] = (o * scale).astype(jnp.bfloat16)
        away = pl.multiple_of(other * 2 * RB, 2 * RB)
        got["rc", j] = send(part.at[j, :, :, pl.ds(away, 2 * RB), :], d2d_in.at[j], to_c)

    home = pl.multiple_of(c * 2 * RB, 2 * RB)
    mine_at = pl.multiple_of((c * 2 + y) * RB, RB)
    theirs_at = pl.multiple_of((c * 2 + 1 - y) * RB, RB)

    def f32(v):
        return v.astype(jnp.float32)

    def r_first(j):
        got["rc", j].wait_recv()
        for s in range(2 * H):
            h, p = s // 2, s % 2
            v = f32(part[j, h, p, pl.ds(home, 2 * RB), :]) + f32(d2d_in[j, h, p])
            part[j, h, p, pl.ds(home, 2 * RB), :] = v.astype(jnp.bfloat16)
        got["ry", j] = send(part.at[j, :, 0, pl.ds(theirs_at, RB), :], y_in.at[j], to_y)
        for d in range(1, H):
            got["rx", j, d] = send(
                part.at[j, (x + d) % H, 1, pl.ds(home, 2 * RB), :], x_in.at[j, d - 1], to_x(d)
            )

    def r_second(j):
        got["ry", j].wait_recv()
        for h in range(H):
            v = f32(part[j, h, 0, pl.ds(mine_at, RB), :]) + f32(y_in[j, h])
            part[j, h, 0, pl.ds(mine_at, RB), :] = v.astype(jnp.bfloat16)
        for d in range(1, H):
            got["rx2", j, d] = send(
                part.at[j, (x + d) % H, 0, pl.ds(mine_at, RB), :], x_in2.at[j, d - 1], to_x(d)
            )
        v = f32(part[j, x, 1, pl.ds(home, 2 * RB), :])
        for d in range(1, H):
            got["rx", j, d].wait_recv()
            v = v + f32(x_in[j, d - 1])
        part[j, x, 1, pl.ds(home, 2 * RB), :] = v.astype(jnp.bfloat16)
        got["ry2", j] = send(part.at[j, x, 1, pl.ds(theirs_at, RB), :], y_in2.at[j], to_y)

    def r_third(j):
        v = f32(part[j, x, 0, pl.ds(mine_at, RB), :])
        for d in range(1, H):
            got["rx2", j, d].wait_recv()
            v = v + f32(x_in2[j, d - 1])
        z_out[j, 0] = v.astype(jnp.bfloat16)
        v = f32(part[j, x, 1, pl.ds(mine_at, RB), :])
        got["ry2", j].wait_recv()
        v = v + f32(y_in2[j])
        z_out[j, 1] = v.astype(jnp.bfloat16)
        if j:
            got["rz", j] = send(z_out.at[j], z_in.at[j - 1], to_z(j))

    stages = [g_start, g_forward, g_pair, compute, r_first, r_second, r_third]
    for t in range(Z + len(stages) - 1):
        for s in reversed(range(len(stages))):
            if 0 <= t - s < Z:
                stages[s](t - s)

    for j in range(1, Z):
        got["rz", j].wait_recv()
    for p in range(2):
        v = f32(z_out[0, p])
        for j in range(1, Z):
            v = v + f32(z_in[j - 1, p])
        out[:, p * WD:(p + 1) * WD] = v.astype(jnp.bfloat16)
    for copy in sent:
        copy.wait_send()


def body(hidden, ids, weights, w_gate, w_up, w_down):
    E = lax.axis_size("expert")
    H = lax.axis_size("head")
    Z = E // 2
    RB, DL = hidden.shape
    WD = DL // 2
    D, F = w_gate.shape[1:]
    rows = E * 2 * RB
    copies = (Z - 1) * 2 + Z * (2 * (H - 1) + 2 + H - 1 + 2 + 1 + 1 + (H - 1) + (H - 1) + 1) + Z - 1
    vmem = pl.BlockSpec(memory_space=pltpu.VMEM)
    anyspace = pl.BlockSpec(memory_space=pl.ANY)
    bf16 = jnp.bfloat16
    X = max(H - 1, 1)
    return pl.pallas_call(
        functools.partial(kernel, (Z, H, RB)),
        out_shape=jax.ShapeDtypeStruct((RB, DL), bf16),
        in_specs=[vmem] * 3 + [anyspace] * 3,
        out_specs=vmem,
        scratch_shapes=[
            pltpu.VMEM((H, 2, rows, WD), bf16),
            pltpu.VMEM((rows, LANES), jnp.float32),
            pltpu.VMEM((D, F), bf16),
            pltpu.VMEM((D, F), bf16),
            pltpu.VMEM((H, 2, F, WD), bf16),
            pltpu.VMEM((Z, H, 2, 4 * RB, WD), bf16),
            pltpu.VMEM((4 * RB, F), bf16),
            pltpu.VMEM((Z, H, 2, 2 * RB, WD), bf16),
            pltpu.VMEM((Z, H, RB, WD), bf16),
            pltpu.VMEM((Z, X, 2 * RB, WD), bf16),
            pltpu.VMEM((Z, X, RB, WD), bf16),
            pltpu.VMEM((Z, RB, WD), bf16),
            pltpu.VMEM((Z, 2, RB, WD), bf16),
            pltpu.VMEM((Z - 1, 2, RB, WD), bf16),
            pltpu.SemaphoreType.DMA((2 + 2 * H,)),
            pltpu.SemaphoreType.DMA((copies,)),
            pltpu.SemaphoreType.DMA((copies,)),
        ],
        compiler_params=pltpu.CompilerParams(
            collective_id=0, has_side_effects=True, vmem_limit_bytes=56 * 1024 * 1024
        ),
    )(hidden, ids, weights, w_gate, w_up, w_down)


def solution(mesh):
    return jax.shard_map(
        body,
        mesh=mesh,
        in_specs=(
            P(("groups", "expert", "pair"), "head"),
            P(("groups", "expert", "pair"), None),
            P(("groups", "expert", "pair"), None),
            P(("expert", "pair"), None, "head"),
            P(("expert", "pair"), None, "head"),
            P(("expert", "pair"), "head", None),
        ),
        out_specs=P(("groups", "expert", "pair"), "head"),
        check_vma=False,
    )
```

time: 261 us -> 63.2 us (0.24)
  the two profiles are of different devices: /device:TPU:13 before, /device:TPU:0 now
where the time goes in v1:
time: 63.2 us; the launch traced here: 63 us
  Pallas kernels  58.7 us (93%)
  local copies, waits for them, and re-layouts  4.29 us (7%)
    pallas_call x1, Pallas kernels, body(): pl.pallas_call(functools.partial(kernel, (Z, H, RB)), out_shape=jax.Shape...  58.7 us
    unnamed x3, local copies, waits for them, and re-layouts  4.29 us

profile of v1, /device:TPU:0, one launch (start us, length us, event | category | flops | bytes accessed | tf_op | source)
XLA Modules:
  0.0 63.0 jit_solution(8872149589406817008)
XLA Ops:
  0.0 1.4 %copy.7.ids = s32[32,8]{1,0:T(8,128)} copy(s32[32,8]{0,1:T(8,128)} %param.7) | data formatting | bytes 2048 | tf_op args[1]
  1.4 1.4 %copy.8.weights = f32[32,8]{1,0:T(8,128)} copy(f32[32,8]{0,1:T(8,128)} %param.8) | data formatting | bytes 2048 | tf_op args[2]
  2.7 58.7 %shard_map.64 = bf16[32,2048]{1,0:T(8,128)(2,1)} custom-call(bf16[32,2048]{1,0:T(8,128)(2,1)} %hidden.1, s32[32,8]{1,0:T(8,128)} %copy.7.ids, f32[32,8]{1,0:T(8,128)} %copy.8.weights, bf16[1,4096,512]{2,1,0:T(8,128)(2,1)} %gate_hbm.1, bf16[1,4096,512]{2,1,0:T(8,128)(2,1)} %up_hbm.1, bf16[1,512,4096]{2,1,0:T(8,128)(2,1)} %down_hbm.1), custom_call_target="tpu_custom_call" | custom-call | tf_op jit(solution)/shard_map/pallas_call | solution.py:239
  61.4 1.6 %copy.10 = bf16[32,2048]{1,0:T(8,128)(2,1)} copy(bf16[32,2048]{1,0:T(8,128)(2,1)} %shard_map.64) | data formatting | bytes 262144

commit v2 on v1

--- a/solution.py
+++ b/solution.py
@@ -23,7 +23,7 @@
 
 def kernel(
     dims, hidden, ids, weights, gate_hbm, up_hbm, down_hbm, out,
-    rows_all, table, w_gate, w_up, w_down, part, act, d2d_in, y_in, x_in, x_in2, y_in2, z_out, z_in,
+    rows_all, table, flipped, w_gate, w_up, w_down, part, act, d2d_in, y_in, x_in, x_in2, y_in2, z_out, z_in,
     w_sem, send_sem, recv_sem,
 ):
     Z, H, RB = dims
@@ -67,11 +67,6 @@
     own = block(z, c, y)
     for p in range(2):
         rows_all[x, p, pl.ds(own, RB), :] = hidden[:, p * WD:(p + 1) * WD]
-    lane = lax.broadcasted_iota(jnp.int32, (RB, LANES), 1)
-    total = jnp.zeros((RB, LANES), jnp.float32)
-    for k in range(ids.shape[1]):
-        total = total + jnp.where(lane == ids[:, k:k + 1], weights[:, k:k + 1], 0.0)
-    table[pl.ds(own, RB), :] = total
 
     barrier = pltpu.get_barrier_semaphore()
     peers = [to_c, to_y] + [to_z(j) for j in range(1, Z)] + [to_x(d) for d in range(1, H)]
@@ -96,19 +91,43 @@
 
     got = {}
 
-    for j in range(1, Z):
-        got["z", j] = same(rows_all.at[x, :, pl.ds(own, RB), :], to_z(j))
-        got["zw", j] = same(table.at[pl.ds(own, RB), :], to_z(j))
+    def z_send(j):
+        if j == 3:
+            at = block(flip(z, 2), c, y)
+            got["z", j] = same(rows_all.at[x, :, pl.ds(at, RB), :], to_z(1))
+        else:
+            got["z", j] = same(rows_all.at[x, :, pl.ds(own, RB), :], to_z(j))
+
+    def make_table():
+        used = 2 * lax.axis_size("expert")
+        line = lax.broadcasted_iota(jnp.int32, (used, RB), 0)
+        total = jnp.zeros((used, RB), jnp.float32)
+        for k in range(ids.shape[0]):
+            total = total + jnp.where(line == ids[k:k + 1, :], weights[k:k + 1, :], 0.0)
+        flipped[...] = jnp.zeros_like(flipped)
+        flipped[:used, :RB] = total
+        table[pl.ds(own, RB), :] = flipped[...].T[:RB, :]
+        for j in range(1, Z):
+            got["zw", j] = same(table.at[pl.ds(own, RB), :], to_z(j))
 
     def g_start(j):
         zc = flip(z, j)
         mine = block(zc, c, y)
-        if j:
+        if j == 0:
+            z_send(1)
+            if Z > 2:
+                z_send(2)
+        else:
             got["z", j].wait_recv()
-        for d in range(1, H):
-            got["x", j, d] = same(rows_all.at[x, :, pl.ds(mine, RB), :], to_x(d))
-        got["y", j] = same(rows_all.at[x, :, pl.ds(mine, RB), :], to_y)
-        if j:
+            if 2 <= j < Z - 1:
+                z_send(j + 1)
+        for p in range(2):
+            for d in range(1, H):
+                got["x", j, d, p] = same(rows_all.at[x, p, pl.ds(mine, RB), :], to_x(d))
+            got["y", j, 1 - p] = same(rows_all.at[x, 1 - p, pl.ds(mine, RB), :], to_y)
+        if j == 0:
+            make_table()
+        else:
             got["zw", j].wait_recv()
         got["yw", j] = same(table.at[pl.ds(mine, RB), :], to_y)
 
@@ -116,26 +135,31 @@
         zc = flip(z, j)
         mine, theirs = block(zc, c, y), block(zc, c, 1 - y)
         for d in range(1, H):
-            got["x", j, d].wait_recv()
+            got["x", j, d, 0].wait_recv()
             got["xy", j, d] = same(rows_all.at[from_x(d), 0, pl.ds(mine, RB), :], to_y)
-        got["y", j].wait_recv()
+        got["y", j, 1].wait_recv()
         for d in range(1, H):
             got["yx", j, d] = same(rows_all.at[x, 1, pl.ds(theirs, RB), :], to_x(d))
 
     def g_pair(j):
         zc = flip(z, j)
-        half = block(zc, c, 0)
+        mine, theirs = block(zc, c, y), block(zc, c, 1 - y)
+        for d in range(1, H):
+            got["x", j, d, 1].wait_recv()
+        got["c", j, 0] = same(rows_all.at[:, :, pl.ds(mine, RB), :], to_c)
+        got["yw", j].wait_recv()
+        got["cw", j] = same(table.at[pl.ds(block(zc, c, 0), 2 * RB), :], to_c)
+        got["y", j, 0].wait_recv()
         for d in range(1, H):
             got["xy", j, d].wait_recv()
             got["yx", j, d].wait_recv()
-        got["yw", j].wait_recv()
-        got["c", j] = same(rows_all.at[:, :, pl.ds(half, 2 * RB), :], to_c)
-        got["cw", j] = same(table.at[pl.ds(half, 2 * RB), :], to_c)
+        got["c", j, 1] = same(rows_all.at[:, :, pl.ds(theirs, RB), :], to_c)
 
     def compute(j):
         zc = flip(z, j)
         start = block(zc, 0, 0)
-        got["c", j].wait_recv()
+        got["c", j, 0].wait_recv()
+        got["c", j, 1].wait_recv()
         got["cw", j].wait_recv()
         if j == 0:
             fetches[0].wait()
@@ -206,11 +230,22 @@
         if j:
             got["rz", j] = send(z_out.at[j], z_in.at[j - 1], to_z(j))
 
-    stages = [g_start, g_forward, g_pair, compute, r_first, r_second, r_third]
-    for t in range(Z + len(stages) - 1):
-        for s in reversed(range(len(stages))):
-            if 0 <= t - s < Z:
-                stages[s](t - s)
+    steps = [(g_start, 0), (g_forward, 0), (g_start, 1)]
+    for j in range(2, Z):
+        steps += [(g_start, j), (g_forward, j - 1), (g_pair, j - 2)]
+        steps += [(compute, j - 3), (r_first, j - 3), (r_second, j - 4), (r_third, j - 5)]
+    n = Z - 1
+    steps += [
+        (g_forward, n), (compute, n - 2), (g_pair, n - 1), (r_first, n - 2), (r_second, n - 3),
+        (compute, n - 1), (g_pair, n), (r_first, n - 1), (r_third, n - 4), (r_second, n - 2), (r_third, n - 3),
+        (compute, n), (r_first, n), (r_third, n - 2), (r_second, n - 1),
+    ]
+    steps = [(f, j) for f, j in steps if j > 0 or (j == 0 and f not in (r_first, r_second, r_third))]
+    steps += [
+        (r_second, n), (r_first, 0), (r_third, n - 1), (r_third, n), (r_second, 0), (r_third, 0),
+    ]
+    for step, j in steps:
+        step(j)
 
     for j in range(1, Z):
         got["rz", j].wait_recv()
@@ -228,10 +263,11 @@
     H = lax.axis_size("head")
     Z = E // 2
     RB, DL = hidden.shape
+    ids, weights = ids.T, weights.T
     WD = DL // 2
     D, F = w_gate.shape[1:]
     rows = E * 2 * RB
-    copies = (Z - 1) * 2 + Z * (2 * (H - 1) + 2 + H - 1 + 2 + 1 + 1 + (H - 1) + (H - 1) + 1) + Z - 1
+    copies = 8 * Z * (H + 2)
     vmem = pl.BlockSpec(memory_space=pltpu.VMEM)
     anyspace = pl.BlockSpec(memory_space=pl.ANY)
     bf16 = jnp.bfloat16
@@ -244,6 +280,7 @@
         scratch_shapes=[
             pltpu.VMEM((H, 2, rows, WD), bf16),
             pltpu.VMEM((rows, LANES), jnp.float32),
+            pltpu.VMEM((LANES, LANES), jnp.float32),
             pltpu.VMEM((D, F), bf16),
             pltpu.VMEM((D, F), bf16),
             pltpu.VMEM((H, 2, F, WD), bf16),

time: 63.2 us -> 58.6 us (0.927)
  local copies, waits for them, and re-layouts: 4.29 us -> 1.57 us
  Pallas kernels: 58.7 us -> 56.8 us
    unnamed x3 -> x1, local copies, waits for them, and re-layouts: 4.29 us -> 1.57 us
    pallas_call x1, Pallas kernels: 58.7 us -> 56.8 us  [body(): pl.pallas_call(functools.partial(kernel, (Z, H, RB)), out_shape=jax.Shape...]
where the time goes in v2:
time: 58.6 us; the launch traced here: 58.4 us
  Pallas kernels  56.8 us (97%)
  local copies, waits for them, and re-layouts  1.57 us (3%)
    pallas_call x1, Pallas kernels, body(): pl.pallas_call(functools.partial(kernel, (Z, H, RB)), out_shape=jax.Shape...  56.8 us
    unnamed x1, local copies, waits for them, and re-layouts  1.57 us

profile of v2, /device:TPU:0, one launch (start us, length us, event | category | flops | bytes accessed | tf_op | source)
XLA Modules:
  0.0 58.4 jit_solution(3344311649874819673)
XLA Ops:
  0.0 56.8 %shard_map.64 = bf16[32,2048]{1,0:T(8,128)(2,1)} custom-call(bf16[32,2048]{1,0:T(8,128)(2,1)} %hidden.1, s32[8,32]{1,0:T(8,128)} %bitcast.2, f32[8,32]{1,0:T(8,128)} %bitcast.3, bf16[1,4096,512]{2,1,0:T(8,128)(2,1)} %gate_hbm.1, bf16[1,4096,512]{2,1,0:T(8,128)(2,1)} %up_hbm.1, bf16[1,512,4096]{2,1,0:T(8,128)(2,1)} %down_hbm.1), custom_call_target="tpu_custom_call" | custom-call | tf_op jit(solution)/shard_map/pallas_call | solution.py:275
  56.8 1.6 %copy.8 = bf16[32,2048]{1,0:T(8,128)(2,1)} copy(bf16[32,2048]{1,0:T(8,128)(2,1)} %shard_map.64) | data formatting | bytes 262144

commit v3 on v2

--- a/solution.py
+++ b/solution.py
@@ -227,8 +227,15 @@
         got["ry2", j].wait_recv()
         v = v + f32(y_in2[j])
         z_out[j, 1] = v.astype(jnp.bfloat16)
-        if j:
+        if j == 3:
+            got["rz", j] = send(z_out.at[j], z_in.at[j - 1], to_z(1))
+        elif j and (j != 2 or Z <= 3):
             got["rz", j] = send(z_out.at[j], z_in.at[j - 1], to_z(j))
+
+    def r_join(j):
+        got["rz", 3].wait_recv()
+        z_out[2] = (f32(z_out[2]) + f32(z_in[2])).astype(jnp.bfloat16)
+        got["rz", 2] = send(z_out.at[2], z_in.at[1], to_z(2))
 
     steps = [(g_start, 0), (g_forward, 0), (g_start, 1)]
     for j in range(2, Z):
@@ -242,16 +249,17 @@
     ]
     steps = [(f, j) for f, j in steps if j > 0 or (j == 0 and f not in (r_first, r_second, r_third))]
     steps += [
-        (r_second, n), (r_first, 0), (r_third, n - 1), (r_third, n), (r_second, 0), (r_third, 0),
+        (r_second, n), (r_first, 0), (r_third, n - 1), (r_third, n), (r_second, 0), (r_join, 0), (r_third, 0),
     ]
     for step, j in steps:
         step(j)
 
-    for j in range(1, Z):
+    direct = [j for j in range(1, Z) if j != 3]
+    for j in direct:
         got["rz", j].wait_recv()
     for p in range(2):
         v = f32(z_out[0, p])
-        for j in range(1, Z):
+        for j in direct:
             v = v + f32(z_in[j - 1, p])
         out[:, p * WD:(p + 1) * WD] = v.astype(jnp.bfloat16)
     for copy in sent:

time: 58.6 us -> 61.4 us (1.048)
  Pallas kernels: 56.8 us -> 59.6 us
    pallas_call x1, Pallas kernels: 56.8 us -> 59.6 us  [body(): pl.pallas_call(functools.partial(kernel, (Z, H, RB)), out_shape=jax.Shape...]
where the time goes in v3:
time: 61.4 us; the launch traced here: 61.2 us
  Pallas kernels  59.6 us (97%)
  local copies, waits for them, and re-layouts  1.57 us (3%)
    pallas_call x1, Pallas kernels, body(): pl.pallas_call(functools.partial(kernel, (Z, H, RB)), out_shape=jax.Shape...  59.6 us
    unnamed x1, local copies, waits for them, and re-layouts  1.57 us

profile of v3, /device:TPU:0, one launch (start us, length us, event | category | flops | bytes accessed | tf_op | source)
XLA Modules:
  0.0 61.2 jit_solution(17354928525272299943)
XLA Ops:
  0.0 59.6 %shard_map.64 = bf16[32,2048]{1,0:T(8,128)(2,1)} custom-call(bf16[32,2048]{1,0:T(8,128)(2,1)} %hidden.1, s32[8,32]{1,0:T(8,128)} %bitcast.2, f32[8,32]{1,0:T(8,128)} %bitcast.3, bf16[1,4096,512]{2,1,0:T(8,128)(2,1)} %gate_hbm.1, bf16[1,4096,512]{2,1,0:T(8,128)(2,1)} %up_hbm.1, bf16[1,512,4096]{2,1,0:T(8,128)(2,1)} %down_hbm.1), custom_call_target="tpu_custom_call" | custom-call | tf_op jit(solution)/shard_map/pallas_call | solution.py:283
  59.6 1.6 %copy.8 = bf16[32,2048]{1,0:T(8,128)(2,1)} copy(bf16[32,2048]{1,0:T(8,128)(2,1)} %shard_map.64) | data formatting | bytes 262144
